TPU v7x, 32 devices: a whole 2x2x4 slice. The times are simulated.
32 devices in a mesh: group: 2 (over y), chan: 4 (over z), tm: 4 (over x, core).
Axes of the slice: x: 2, y: 2, z: 4, core: 2. Of those that a mesh axis runs over, the one named last changes fastest.
Arguments:
- samples: bfloat16 [8192, 1024], P(('group', 'tm'), 'chan'), parts along dimension 0, may hold values from -6 to 6
- pair_mask: int32 [8, 4], P(('group', 'chan')), parts along dimension 0, may hold values 0 or 1
Outputs:
- cross_cov: float32 [32, 2048, 1024], P('tm', ('group', 'chan')), parts along dimension 1
There are 2 independent parts, one for each index of `group`. A program takes and returns all parts, laid end to end along the dimension named above; each array names one. Nothing has to cross between parts.
All inputs are finite; a program needn't handle non-finite values. No bound on the sum of `pair_mask` on one device may be relied on, other than what follows from the above.
Results may differ from a plain program's by a relative error of at most 0.0003.
Values may be sent and summed in bfloat16 or wider, within the bound.
A program may use at most 128 MiB of HBM per device.

v0:
```python
import jax
import jax.numpy as jnp
from jax import lax
from jax.sharding import PartitionSpec as P

LAGS = 32
STEPS = 4


def from_behind(value, axis, steps):
    count = lax.axis_size(axis)
    pairs = [(source, (source + steps) % count) for source in range(count)]
    return lax.ppermute(value, axis, pairs)


def cycle_partners(block):
    partners = [block]
    moving = block
    for step in range(1, STEPS):
        moving = from_behind(moving, "chan", -1)
        partners.append(moving)
    return partners


def lagged_product(stacked, partner, flag, count, width):

    def compute():
        product = lax.dot_general(
            stacked, partner, (((0,), (0,)), ((), ())), preferred_element_type=jnp.float32
        )
        return product.reshape(count, width, width)

    def nothing():
        return jnp.zeros((count, width, width), jnp.float32)

    return lax.cond(flag > 0, compute, nothing)


def shards(samples, pair_mask):
    width = samples.shape[1]
    slabs = lax.axis_size("tm")
    lag_dev = LAGS // slabs
    flags = pair_mask[0]
    time_total = samples.shape[0] * slabs
    series = lax.all_gather(samples, "tm", axis=0, tiled=True)
    partners = cycle_partners(series)
    length = series.shape[0]
    first = lax.axis_index("tm") * lag_dev
    padded = jnp.concatenate([series, jnp.zeros((LAGS, width), series.dtype)], axis=0)
    stacked = jnp.concatenate(
        [lax.dynamic_slice_in_dim(padded, first + j, length, 0) for j in range(lag_dev)], axis=1
    )
    raw = jnp.concatenate(
        [
            lagged_product(stacked, partners[step], flags[step], lag_dev, width)
            for step in range(STEPS)
        ],
        axis=2,
    )
    return raw / jnp.sqrt(jnp.float32(time_total))


def solution(mesh):
    placed = (P(("group", "tm"), "chan"), P(("group", "chan"), None))
    return jax.shard_map(
        shards,
        mesh=mesh,
        in_specs=placed,
        out_specs=P("tm", ("group", "chan"), None),
        check_vma=False,
    )
```

profile of v0, /device:TPU:1, one launch (start us, length us, event | category | flops | bytes accessed | tf_op | source)
XLA Modules:
  0.0 203.0 jit_solution(13999915298820558987)
XLA Ops:
  6.5 0.0 all-gather.2.cloned.1.call-start
  6.5 0.7 all-gather.2.cloned.1.call-update
  7.3 26.8 %all-gather.2.cloned.1.call-done = bf16[4096,256]{1,0:T(8,128)(2,1)} async-done(((bf16[1024,256]{1,0:T(8,128)(2,1)}), bf16[4096,256]{1,0:T(8,128)(2,1)}) %all-gather.2.cloned.1.call-update) | async-done | bytes 2097168 | tf_op jit(solution)/shard_map/all_gather | solution.py:45
  34.0 3.0 %collective-permute-start = (bf16[4096,256]{1,0:T(8,128)(2,1)}, bf16[4096,256]{1,0:T(8,128)(2,1)}, u32[]{:S(2)}, u32[]{:S(2)}) collective-permute-start(bf16[4096,256]{1,0:T(8,128)(2,1)} %all-gather.2.cloned.1.call-done), channel_id=1, source_target_pairs={{0,12},{4,0},{8,4},{12,8},{1,13},{5,1},{9,5},{13,9},{2,14},{6,2},{... | collective-permute-start | bytes 6291464 | tf_op jit(solution)/shard_map/ppermute | solution.py:13
  37.1 45.1 %collective-permute-done = bf16[4096,256]{1,0:T(8,128)(2,1)} collective-permute-done((bf16[4096,256]{1,0:T(8,128)(2,1)}, bf16[4096,256]{1,0:T(8,128)(2,1)}, u32[]{:S(2)}, u32[]{:S(2)}) %collective-permute-start) | collective-permute-done | bytes 2097184 | tf_op jit(solution)/shard_map/ppermute | solution.py:13
  82.1 4.0 %collective-permute-start.1 = (bf16[4096,256]{1,0:T(8,128)(2,1)}, bf16[4096,256]{1,0:T(8,128)(2,1)}, u32[]{:S(2)}, u32[]{:S(2)}) collective-permute-start(bf16[4096,256]{1,0:T(8,128)(2,1)} %collective-permute-done), channel_id=1, source_target_pairs={{0,12},{4,0},{8,4},{12,8},{1,13},{5,1},{9,5},{13,9},{2,14},{6,2},{... | collective-permute-start | bytes 6291464 | tf_op jit(solution)/shard_map/ppermute | solution.py:13
  86.1 1.5 fusion
  88.2 0.0 copy-start
  90.3 3.2 %dynamic-slice_dynamic-update-slice_fusion.7 = bf16[4096,2048]{1,0:T(8,128)(2,1)} fusion(s32[]{:T(128)S(6)} %select_n.24, bf16[4096,256]{1,0:T(8,128)(2,1)} %all-gather.2.cloned.1.call-done), kind=kLoop, calls=%fused_computation.8 | loop fusion | bytes 4194308
  93.4 0.0 copy-done
  93.4 2.0 dynamic-slice_dynamic-update-slice_fusion.6
  95.4 1.9 dynamic-slice_dynamic-update-slice_fusion.5
  97.3 33.0 %collective-permute-done.1 = bf16[4096,256]{1,0:T(8,128)(2,1)} collective-permute-done((bf16[4096,256]{1,0:T(8,128)(2,1)}, bf16[4096,256]{1,0:T(8,128)(2,1)}, u32[]{:S(2)}, u32[]{:S(2)}) %collective-permute-start.1) | collective-permute-done | bytes 2097184 | tf_op jit(solution)/shard_map/ppermute | solution.py:13
  130.3 4.0 %collective-permute-start.2 = (bf16[4096,256]{1,0:T(8,128)(2,1)}, bf16[4096,256]{1,0:T(8,128)(2,1)}, u32[]{:S(2)}, u32[]{:S(2)}) collective-permute-start(bf16[4096,256]{1,0:T(8,128)(2,1)} %collective-permute-done.1), channel_id=1, source_target_pairs={{0,12},{4,0},{8,4},{12,8},{1,13},{5,1},{9,5},{13,9},{2,14},{6,2},{... | collective-permute-start | bytes 6291464 | tf_op jit(solution)/shard_map/ppermute | solution.py:13
  134.3 1.9 dynamic-slice_dynamic-update-slice_fusion.4
  136.2 2.0 dynamic-slice_dynamic-update-slice_fusion.3
  138.2 1.9 dynamic-slice_dynamic-update-slice_fusion.2
  140.1 1.9 dynamic-slice_dynamic-update-slice_fusion.1
  142.0 1.9 dynamic-slice_dynamic-update-slice_fusion
  143.9 9.7 %conditional.4 = (f32[8,256,256]{2,1,0:T(8,128)}) conditional(s32[]{:T(128)} %bitcast.4, () %tuple.29, (bf16[4096,2048]{1,0:T(8,128)(2,1)}, bf16[4096,256]{1,0:T(8,128)(2,1)S(1)}) %tuple.50), branch_computations={%region_0.0_spmd, %region_1.0_spmd} | conditional | flops 4294967296 | bytes 20971528 | solution.py:36
  143.9 9.7 %fusion.1 = f32[2048,256]{1,0:T(8,128)} fusion(bf16[4096,2048]{1,0:T(8,128)(2,1)} %get-tuple-element.28, bf16[4096,256]{1,0:T(8,128)(2,1)S(1)} %get-tuple-element.32), kind=kOutput, calls=%fused_computation.10 | convolution fusion | flops 4294967296 | bytes 20971520 | tf_op jit(solution)/shard_map/cond/branch_1_fun/dot_general | solution.py:28
  153.6 8.7 %conditional.5 = (f32[8,256,256]{2,1,0:T(8,128)S(1)}) conditional(s32[]{:T(128)} %bitcast.5, () %tuple.31, (bf16[4096,2048]{1,0:T(8,128)(2,1)}, bf16[4096,256]{1,0:T(8,128)(2,1)}) %tuple.32), branch_computations={%region_2.0_spmd, %region_3.0_spmd} | conditional | flops 4294967296 | bytes 20971528 | solution.py:36
  153.6 8.7 %fusion.2 = f32[2048,256]{1,0:T(8,128)S(1)} fusion(bf16[4096,2048]{1,0:T(8,128)(2,1)} %get-tuple-element.34, bf16[4096,256]{1,0:T(8,128)(2,1)} %get-tuple-element.36), kind=kOutput, calls=%fused_computation.11 | convolution fusion | flops 4294967296 | bytes 20971520 | tf_op jit(solution)/shard_map/cond/branch_1_fun/dot_general | solution.py:28
  162.4 12.8 %conditional.6 = (f32[8,256,256]{2,1,0:T(8,128)}) conditional(s32[]{:T(128)} %bitcast.6, () %tuple.33, (bf16[4096,2048]{1,0:T(8,128)(2,1)}, bf16[4096,256]{1,0:T(8,128)(2,1)}) %tuple.34), branch_computations={%region_4.0_spmd, %region_5.0_spmd} | conditional | flops 4294967296 | bytes 20971528 | solution.py:36
  162.6 12.6 %fusion.3 = f32[2048,256]{1,0:T(8,128)} fusion(bf16[4096,2048]{1,0:T(8,128)(2,1)} %get-tuple-element.37, bf16[4096,256]{1,0:T(8,128)(2,1)} %get-tuple-element.38), kind=kOutput, calls=%fused_computation.12 | convolution fusion | flops 4294967296 | bytes 20971520 | tf_op jit(solution)/shard_map/cond/branch_1_fun/dot_general | solution.py:28
  175.2 2.3 %collective-permute-done.2 = bf16[4096,256]{1,0:T(8,128)(2,1)} collective-permute-done((bf16[4096,256]{1,0:T(8,128)(2,1)}, bf16[4096,256]{1,0:T(8,128)(2,1)}, u32[]{:S(2)}, u32[]{:S(2)}) %collective-permute-start.2) | collective-permute-done | bytes 2097184 | tf_op jit(solution)/shard_map/ppermute | solution.py:13
  177.5 12.6 %conditional.7 = (f32[8,256,256]{2,1,0:T(8,128)}) conditional(s32[]{:T(128)} %bitcast.7, () %tuple.35, (bf16[4096,2048]{1,0:T(8,128)(2,1)}, bf16[4096,256]{1,0:T(8,128)(2,1)}) %tuple.36), branch_computations={%region_6.0_spmd, %region_7.0_spmd} | conditional | flops 4294967296 | bytes 20971528 | solution.py:36
  177.5 12.6 %fusion.4 = f32[2048,256]{1,0:T(8,128)} fusion(bf16[4096,2048]{1,0:T(8,128)(2,1)} %get-tuple-element.39, bf16[4096,256]{1,0:T(8,128)(2,1)} %get-tuple-element.40), kind=kOutput, calls=%fused_computation.13 | convolution fusion | flops 4294967296 | bytes 20971520 | tf_op jit(solution)/shard_map/cond/branch_1_fun/dot_general | solution.py:28
  190.2 6.0 %maximum_multiply_fusion = f32[8,256,1024]{2,1,0:T(8,128)} fusion(f32[8,256,256]{2,1,0:T(8,128)} %get-tuple-element.48, f32[8,256,256]{2,1,0:T(8,128)} %get-tuple-element.47, f32[8,256,256]{2,1,0:T(8,128)S(1)} %get-tuple-element.46, f32[8,256,256]{2,1,0:T(8,128)} %get-tuple-element.45), kind=kLoop, calls=%fused_computation | loop fusion | flops 8388608 | bytes 16777216 | tf_op jit(solution)/shard_map/div | solution.py:60
Async XLA Ops:
  6.5 27.5 %all-gather.2.cloned.1.call-start = ((), (), s32[]{:S(2)}) async-start(), calls=%async_computation | async-start | bytes 2621440 | tf_op jit(solution)/shard_map/all_gather | solution.py:45
  34.0 48.1 %collective-permute-start = (bf16[4096,256]{1,0:T(8,128)(2,1)}, bf16[4096,256]{1,0:T(8,128)(2,1)}, u32[]{:S(2)}, u32[]{:S(2)}) collective-permute-start(bf16[4096,256]{1,0:T(8,128)(2,1)} %all-gather.2.cloned.1.call-done), channel_id=1, source_target_pairs={{0,12},{4,0},{8,4},{12,8},{1,13},{5,1},{9,5},{13,9},{2,14},{6,2},{... | collective-permute-start | bytes 6291464 | tf_op jit(solution)/shard_map/ppermute | solution.py:13
  82.1 48.1 %collective-permute-start.1 = (bf16[4096,256]{1,0:T(8,128)(2,1)}, bf16[4096,256]{1,0:T(8,128)(2,1)}, u32[]{:S(2)}, u32[]{:S(2)}) collective-permute-start(bf16[4096,256]{1,0:T(8,128)(2,1)} %collective-permute-done), channel_id=1, source_target_pairs={{0,12},{4,0},{8,4},{12,8},{1,13},{5,1},{9,5},{13,9},{2,14},{6,2},{... | collective-permute-start | bytes 6291464 | tf_op jit(solution)/shard_map/ppermute | solution.py:13
  88.2 5.2 %copy-start = (bf16[4096,256]{1,0:T(8,128)(2,1)S(1)}, bf16[4096,256]{1,0:T(8,128)(2,1)}, u32[]{:S(2)}) copy-start(bf16[4096,256]{1,0:T(8,128)(2,1)} %all-gather.2.cloned.1.call-done) | copy-start | bytes 6291460
  130.3 47.2 %collective-permute-start.2 = (bf16[4096,256]{1,0:T(8,128)(2,1)}, bf16[4096,256]{1,0:T(8,128)(2,1)}, u32[]{:S(2)}, u32[]{:S(2)}) collective-permute-start(bf16[4096,256]{1,0:T(8,128)(2,1)} %collective-permute-done.1), channel_id=1, source_target_pairs={{0,12},{4,0},{8,4},{12,8},{1,13},{5,1},{9,5},{13,9},{2,14},{6,2},{... | collective-permute-start | bytes 6291464 | tf_op jit(solution)/shard_map/ppermute | solution.py:13
Sparse Core Ops, SparseCore 0:
  8.9 25.0 all-gather.1
where the time goes:
time: 206 us; the launch traced here: 203 us
  waiting for transfers between devices  108 us (52%)
  matrix products  43.7 us (21%)
  local copies, waits for them, and re-layouts  18.1 us (9%)
  between operations  16.1 us (8%)
  starting transfers between devices  11 us (5%)
  other arithmetic  5.96 us (3%)
    ppermute x3, waiting for transfers between devices, from_behind(): return lax.ppermute(value, axis, pairs)  80.3 us
    dot_general x4, matrix products, compute(): lax.dot_general(stacked, partner, (((0,), (0,)), ((), ())), preferred_ele...  43.7 us
    all_gather x1, waiting for transfers between devices, shards(): series = lax.all_gather(samples, 'tm', axis=0, tiled=True)  26.8 us
    unnamed x9, local copies, waits for them, and re-layouts  14.8 us
    ppermute x3, starting transfers between devices, from_behind(): return lax.ppermute(value, axis, pairs)  11 us
    div x1, other arithmetic, shards(): return raw / jnp.sqrt(jnp.float32(time_total))  5.96 us
  transfers between devices with their start and end apart: 4, of which 4 were waited for; matrix products, arithmetic and copies ran while one was open for 24% of the time, Pallas kernels for 0%

commit v1 on v0

--- a/solution.py
+++ b/solution.py
@@ -1,10 +1,15 @@
+import functools
+
 import jax
 import jax.numpy as jnp
 from jax import lax
+from jax.experimental import pallas as pl
+from jax.experimental.pallas import tpu as pltpu
 from jax.sharding import PartitionSpec as P
 
 LAGS = 32
 STEPS = 4
+PIECES = 2
 
 
 def from_behind(value, axis, steps):
@@ -60,10 +65,273 @@
     return raw / jnp.sqrt(jnp.float32(time_total))
 
 
+def kernel(slab, width, lags, flags, own, out, got, wide, stack, total,
+           own_sem, out_sem, send_sem, recv_sem):
+    z = lax.axis_index("chan")
+    m = lax.axis_index("tm")
+    x, core = m // 2, m % 2
+    other = 1 - x
+    last = STEPS - 1
+    end = (z == 0) | (z == last)
+    mid = (z > 0) & (z < last)
+    twin = z + 1 - 2 * (z % 2)
+    sibling = {"tm": 2 * x + 1 - core}
+    across = {"tm": 2 * other + core}
+    up, down = {"chan": z + 1}, {"chan": z - 1}
+    rows = slab // PIECES
+    length = 4 * slab
+    factor = 1.0 / (float(length) ** 0.5)
+    high = z // 2
+    low = z % 2
+    near = 1 + low
+    far = 3 * (1 - high)
+    middle = 6 - z - near - far
+    sent = []
+
+    def home(zp, xp, plane, h, count=1):
+        begin = pl.multiple_of((2 * xp + plane) * slab + h * rows, rows)
+        return got.at[zp, pl.ds(begin, count * rows), :]
+
+    def send(cond, way, target, zp, xp, h):
+        piece = home(zp, xp, core, h)
+        copy = pltpu.make_async_remote_copy(
+            src_ref=piece,
+            dst_ref=piece,
+            send_sem=send_sem.at[way, zp, xp, h],
+            recv_sem=recv_sem.at[zp, 2 * xp + core, h],
+            device_id=target,
+            device_id_type=pl.DeviceIdType.MESH,
+        )
+        if cond is None:
+            copy.start()
+        else:
+            pl.when(cond)(copy.start)
+        return cond, copy
+
+    def arrive(zp, xp, plane, h):
+        piece = home(zp, xp, plane, h)
+        pltpu.make_async_copy(piece, piece, recv_sem.at[zp, 2 * xp + plane, h]).wait()
+
+    def from_z(r, h):
+        for d in (1, -1):
+            zp = z + d * r
+            here = (zp >= 0) & (zp <= last)
+            zq = jnp.clip(zp, 0, last)
+
+            @pl.when(here)
+            def _():
+                arrive(zq, x, core, h)
+
+            onward = (z > 0) if d == 1 else (z < last)
+            sent.append(send(here & onward, 0 if d == 1 else 1, down if d == 1 else up, zq, x, h))
+            skip = (zp == twin) if h >= PIECES // 2 else ((zp == twin) & mid)
+            sent.append(send(here & jnp.logical_not(skip), 2, across, zq, x, h))
+            sent.append(send(here, 3, sibling, zq, x, h))
+
+    def lend(h, cond):
+        sent.append(send(cond & (low == 0), 1, up, z, other, h))
+        sent.append(send(cond & (low == 1), 0, down, z, other, h))
+
+    def from_x(zp, h):
+        arrive(zp, other, core, h)
+        sent.append(send(None, 3, sibling, zp, other, h))
+
+    def from_sibling(zp, xp, h):
+        arrive(zp, xp, 1 - core, h)
+
+    tall = 4 * width
+
+    def product(zp, begin, depth, fresh=False, scaled=False):
+        step = (zp - z + STEPS) % STEPS
+        begin = pl.multiple_of(begin, rows)
+
+        def body(i, carry):
+            lines = pl.ds(pl.multiple_of(i * tall, tall), tall)
+            value = jnp.dot(
+                stack[lines, pl.ds(begin, depth)],
+                got[zp, pl.ds(begin, depth), :],
+                preferred_element_type=jnp.float32,
+            )
+            if not fresh:
+                value = total[step, lines, :] + value
+            if scaled:
+                value = value * (flags[0, step].astype(jnp.float32) * factor)
+            total[step, lines, :] = value
+            return carry
+
+        lax.fori_loop(0, lags * width // tall, body, 0)
+
+    def emit(zp):
+        step = (zp - z + STEPS) % STEPS
+        copies = []
+        for j in range(lags):
+            copy = pltpu.make_async_copy(
+                total.at[step, pl.ds(j * width, width), :],
+                out.at[j, :, pl.ds(pl.multiple_of(step * width, width), width)],
+                out_sem.at[step, j],
+            )
+            copy.start()
+            copies.append(copy)
+        return copies
+
+    load = pltpu.make_async_copy(own, got.at[z, pl.ds(pl.multiple_of(m * slab, slab), slab), :], own_sem)
+    load.start()
+
+    barrier = pltpu.get_barrier_semaphore()
+    for target, cond in ((sibling, None), (across, None), (up, z < last), (down, z > 0)):
+        def greet(target=target):
+            pl.semaphore_signal(barrier, inc=1, device_id=target, device_id_type=pl.DeviceIdType.MESH)
+        if cond is None:
+            greet()
+        else:
+            pl.when(cond)(greet)
+    pl.semaphore_wait(barrier, jnp.where(mid, 4, 3))
+    load.wait()
+
+    for h in range(PIECES):
+        sent.append(send(z > 0, 0, down, z, x, h))
+        sent.append(send(z < last, 1, up, z, x, h))
+        sent.append(send(None, 2, across, z, x, h))
+        sent.append(send(None, 3, sibling, z, x, h))
+
+    for h in range(PIECES):
+        from_x(z, h)
+        lend(h, end)
+        from_z(1, h)
+
+    for h in range(PIECES):
+        from_sibling(z, x, h)
+        from_sibling(z, other, h)
+
+    part = 512
+
+    def widen(i, carry):
+        at = pl.ds(pl.multiple_of(i * part, part), part)
+        wide[at, :] = got[z, at, :].astype(jnp.float32)
+        return carry
+
+    lax.fori_loop(0, length // part, widen, 0)
+    wide[pl.ds(length, LAGS), :] = jnp.zeros((LAGS, width), jnp.float32)
+
+    def shift(i, carry):
+        begin = pl.multiple_of(i * part, part)
+        base = wide[pl.ds(pl.multiple_of(begin + m * lags, 8), part + 8), :]
+        for j in range(lags):
+            moved = base[j:j + part, :].astype(jnp.bfloat16)
+            stack[pl.ds(j * width, width), pl.ds(begin, part)] = moved.T
+        return carry
+
+    lax.fori_loop(0, length // part, shift, 0)
+
+    half = 2 * slab
+    from_z(2, 0)
+    product(z, 0, half, fresh=True)
+    product(z, half, half, scaled=True)
+    written = emit(z)
+
+    for h in range(1, PIECES):
+        from_z(2, h)
+    for h in range(PIECES // 2, PIECES):
+        lend(h, mid)
+    for h in range(PIECES // 2):
+        from_x(near, h)
+    for h in range(PIECES):
+        from_sibling(near, x, h)
+    product(near, x * half, half, fresh=True)
+    for h in range(PIECES):
+        from_sibling(middle, x, h)
+    product(middle, x * half, half, fresh=True)
+
+    from_z(3, 0)
+    for h in range(PIECES):
+        from_x(middle, h)
+    for h in range(PIECES):
+        from_sibling(middle, other, h)
+    product(middle, other * half, half, scaled=True)
+    written += emit(middle)
+
+    for h in range(1, PIECES):
+        from_z(3, h)
+    for h in range(PIECES):
+        from_sibling(far, x, h)
+    product(far, x * half, half, fresh=True)
+
+    early = PIECES // 2
+    depth = early * rows
+    mine = (2 * other + core) * slab
+    theirs = (2 * other + 1 - core) * slab
+    for h in range(early):
+        from_sibling(near, other, h)
+    product(near, mine, depth)
+    product(near, theirs, depth)
+    for h in range(early):
+        from_x(far, h)
+    product(far, mine, depth)
+    for h in range(early):
+        from_sibling(far, other, h)
+    product(far, theirs, depth)
+    for h in range(early, PIECES):
+        from_x(near, h)
+        from_x(far, h)
+    product(near, mine + depth, depth)
+    product(far, mine + depth, depth)
+    for h in range(early, PIECES):
+        from_sibling(near, other, h)
+    product(near, theirs + depth, depth, scaled=True)
+    written += emit(near)
+    for h in range(early, PIECES):
+        from_sibling(far, other, h)
+    product(far, theirs + depth, depth, scaled=True)
+    written += emit(far)
+
+    for cond, copy in sent:
+        if cond is None:
+            copy.wait_send()
+        else:
+            pl.when(cond)(copy.wait_send)
+    for copy in written:
+        copy.wait()
+
+
+def fused(samples, pair_mask):
+    slab, width = samples.shape
+    slabs = lax.axis_size("tm")
+    lags = LAGS // slabs
+    length = slab * slabs
+    return pl.pallas_call(
+        functools.partial(kernel, slab, width, lags),
+        out_shape=jax.ShapeDtypeStruct((lags, width, STEPS * width), jnp.float32),
+        in_specs=[
+            pl.BlockSpec(memory_space=pltpu.SMEM),
+            pl.BlockSpec(memory_space=pl.ANY),
+        ],
+        out_specs=pl.BlockSpec(memory_space=pl.ANY),
+        scratch_shapes=[
+            pltpu.VMEM((STEPS, length, width), samples.dtype),
+            pltpu.VMEM((length + LAGS, width), jnp.float32),
+            pltpu.VMEM((lags * width, length), samples.dtype),
+            pltpu.VMEM((STEPS, lags * width, width), jnp.float32),
+            pltpu.SemaphoreType.DMA,
+            pltpu.SemaphoreType.DMA((STEPS, lags)),
+            pltpu.SemaphoreType.DMA((4, STEPS, 2, PIECES)),
+            pltpu.SemaphoreType.DMA((STEPS, slabs, PIECES)),
+        ],
+        compiler_params=pltpu.CompilerParams(
+            collective_id=0, has_side_effects=True, vmem_limit_bytes=56 * 1024 * 1024
+        ),
+        cost_estimate=pl.CostEstimate(
+            flops=2 * lags * width * STEPS * width * length,
+            bytes_accessed=4 * lags * width * STEPS * width,
+            transcendentals=0,
+        ),
+    )(pair_mask, samples)
+
+
 def solution(mesh):
     placed = (P(("group", "tm"), "chan"), P(("group", "chan"), None))
+    whole_cycle = mesh.shape["chan"] == STEPS and mesh.shape["tm"] == 4
     return jax.shard_map(
-        shards,
+        fused if whole_cycle else shards,
         mesh=mesh,
         in_specs=placed,
         out_specs=P("tm", ("group", "chan"), None),

time: 206 us -> 64 us (0.31); the launches traced: 203 us -> 63.9 us
  waiting for transfers between devices: 108 us -> 0 us
  Pallas kernels: 0 us -> 55.4 us
  matrix products: 43.7 us -> 0 us
  between operations: 16.1 us -> 0.01 us
  starting transfers between devices: 11 us -> 0 us
  local copies, waits for them, and re-layouts: 18.1 us -> 8.44 us
  other arithmetic: 5.96 us -> 0 us
    ppermute x3 -> x0, waiting for transfers between devices: 80.3 us -> none  [from_behind(): return lax.ppermute(value, axis, pairs)]
    pallas_call x0 -> x1, Pallas kernels: none -> 55.4 us  [fused(): pl.pallas_call(functools.partial(kernel, slab, width, lags), out_shape=ja...]
    dot_general x4 -> x0, matrix products: 43.7 us -> none  [compute(): lax.dot_general(stacked, partner, (((0,), (0,)), ((), ())), preferred_ele...]
    all_gather x1 -> x0, waiting for transfers between devices: 26.8 us -> none  [shards(): series = lax.all_gather(samples, 'tm', axis=0, tiled=True)]
    ppermute x3 -> x0, starting transfers between devices: 11 us -> none  [from_behind(): return lax.ppermute(value, axis, pairs)]
    unnamed x9 -> x1, local copies, waits for them, and re-layouts: 14.8 us -> 8.44 us
    div x1 -> x0, other arithmetic: 5.96 us -> none  [shards(): return raw / jnp.sqrt(jnp.float32(time_total))]
  transfers between devices with their start and end apart: 4 -> 0, of which waited for: 4 -> 0; matrix products, arithmetic and copies ran while one was open for 24% -> 0% of each run, Pallas kernels for 0% -> 0%
where the time goes in v1:
time: 64 us; the launch traced here: 63.9 us
  Pallas kernels  55.4 us (87%)
  local copies, waits for them, and re-layouts  8.44 us (13%)
    pallas_call x1, Pallas kernels, fused(): pl.pallas_call(functools.partial(kernel, slab, width, lags), out_shape=ja...  55.4 us
    unnamed x1, local copies, waits for them, and re-layouts  8.44 us

profile of v1, /device:TPU:1, one launch (start us, length us, event | category | flops | bytes accessed | tf_op | source)
XLA Modules:
  0.0 63.9 jit_solution(8628619242936359115)
XLA Ops:
  0.0 55.4 %shard_map.28 = f32[8,256,1024]{2,1,0:T(8,128)} custom-call(s32[1,4]{1,0:T(1,128)} %flags.1, bf16[1024,256]{1,0:T(8,128)(2,1)} %own.1), custom_call_target="tpu_custom_call" | custom-call | flops 17179869184 | bytes 8388608 | tf_op jit(solution)/shard_map/pallas_call | solution.py:301
  55.4 8.4 %copy.4 = f32[8,256,1024]{2,1,0:T(8,128)} copy(f32[8,256,1024]{2,1,0:T(8,128)} %shard_map.28) | data formatting | bytes 16777216

commit v2 on v1

--- a/solution.py
+++ b/solution.py
@@ -65,8 +65,8 @@
     return raw / jnp.sqrt(jnp.float32(time_total))
 
 
-def kernel(slab, width, lags, flags, own, out, got, wide, stack, total,
-           own_sem, out_sem, send_sem, recv_sem):
+def kernel(slab, width, lags, flags, own, out, got, wide, stack,
+           own_sem, send_sem, recv_sem):
     z = lax.axis_index("chan")
     m = lax.axis_index("tm")
     x, core = m // 2, m % 2
@@ -139,11 +139,13 @@
     def from_sibling(zp, xp, h):
         arrive(zp, xp, 1 - core, h)
 
-    tall = 4 * width
+    group = 4
+    tall = group * width
 
     def product(zp, begin, depth, fresh=False, scaled=False):
         step = (zp - z + STEPS) % STEPS
         begin = pl.multiple_of(begin, rows)
+        columns = pl.ds(pl.multiple_of(step * width, width), width)
 
         def body(i, carry):
             lines = pl.ds(pl.multiple_of(i * tall, tall), tall)
@@ -152,27 +154,16 @@
                 got[zp, pl.ds(begin, depth), :],
                 preferred_element_type=jnp.float32,
             )
+            value = value.reshape(group, width, width)
+            place = (pl.ds(i * group, group), slice(None), columns)
             if not fresh:
-                value = total[step, lines, :] + value
+                value = out[place] + value
             if scaled:
                 value = value * (flags[0, step].astype(jnp.float32) * factor)
-            total[step, lines, :] = value
+            out[place] = value
             return carry
 
-        lax.fori_loop(0, lags * width // tall, body, 0)
-
-    def emit(zp):
-        step = (zp - z + STEPS) % STEPS
-        copies = []
-        for j in range(lags):
-            copy = pltpu.make_async_copy(
-                total.at[step, pl.ds(j * width, width), :],
-                out.at[j, :, pl.ds(pl.multiple_of(step * width, width), width)],
-                out_sem.at[step, j],
-            )
-            copy.start()
-            copies.append(copy)
-        return copies
+        lax.fori_loop(0, lags // group, body, 0)
 
     load = pltpu.make_async_copy(own, got.at[z, pl.ds(pl.multiple_of(m * slab, slab), slab), :], own_sem)
     load.start()
@@ -227,7 +218,6 @@
     from_z(2, 0)
     product(z, 0, half, fresh=True)
     product(z, half, half, scaled=True)
-    written = emit(z)
 
     for h in range(1, PIECES):
         from_z(2, h)
@@ -248,7 +238,6 @@
     for h in range(PIECES):
         from_sibling(middle, other, h)
     product(middle, other * half, half, scaled=True)
-    written += emit(middle)
 
     for h in range(1, PIECES):
         from_z(3, h)
@@ -278,19 +267,15 @@
     for h in range(early, PIECES):
         from_sibling(near, other, h)
     product(near, theirs + depth, depth, scaled=True)
-    written += emit(near)
     for h in range(early, PIECES):
         from_sibling(far, other, h)
     product(far, theirs + depth, depth, scaled=True)
-    written += emit(far)
 
     for cond, copy in sent:
         if cond is None:
             copy.wait_send()
         else:
             pl.when(cond)(copy.wait_send)
-    for copy in written:
-        copy.wait()
 
 
 def fused(samples, pair_mask):
@@ -300,24 +285,22 @@
     length = slab * slabs
     return pl.pallas_call(
         functools.partial(kernel, slab, width, lags),
-        out_shape=jax.ShapeDtypeStruct((lags, width, STEPS * width), jnp.float32),
+        out_shape=pltpu.VMEM((lags, width, STEPS * width), jnp.float32),
         in_specs=[
             pl.BlockSpec(memory_space=pltpu.SMEM),
             pl.BlockSpec(memory_space=pl.ANY),
         ],
-        out_specs=pl.BlockSpec(memory_space=pl.ANY),
+        out_specs=pl.BlockSpec(memory_space=pltpu.VMEM),
         scratch_shapes=[
             pltpu.VMEM((STEPS, length, width), samples.dtype),
             pltpu.VMEM((length + LAGS, width), jnp.float32),
             pltpu.VMEM((lags * width, length), samples.dtype),
-            pltpu.VMEM((STEPS, lags * width, width), jnp.float32),
             pltpu.SemaphoreType.DMA,
-            pltpu.SemaphoreType.DMA((STEPS, lags)),
             pltpu.SemaphoreType.DMA((4, STEPS, 2, PIECES)),
             pltpu.SemaphoreType.DMA((STEPS, slabs, PIECES)),
         ],
         compiler_params=pltpu.CompilerParams(
-            collective_id=0, has_side_effects=True, vmem_limit_bytes=56 * 1024 * 1024
+            collective_id=0, has_side_effects=True, vmem_limit_bytes=48 * 1024 * 1024
         ),
         cost_estimate=pl.CostEstimate(
             flops=2 * lags * width * STEPS * width * length,

time: 64 us -> 57.4 us (0.90)
  local copies, waits for them, and re-layouts: 8.44 us -> 3.4 us
  Pallas kernels: 55.4 us -> 53.9 us
    unnamed x1, local copies, waits for them, and re-layouts: 8.44 us -> 3.4 us
    pallas_call x1, Pallas kernels: 55.4 us -> 53.9 us  [fused(): pl.pallas_call(functools.partial(kernel, slab, width, lags), out_shape=pl...]
where the time goes in v2:
time: 57.4 us; the launch traced here: 57.3 us
  Pallas kernels  53.9 us (94%)
  local copies, waits for them, and re-layouts  3.4 us (6%)
    pallas_call x1, Pallas kernels, fused(): pl.pallas_call(functools.partial(kernel, slab, width, lags), out_shape=pl...  53.9 us
    unnamed x1, local copies, waits for them, and re-layouts  3.4 us

profile of v2, /device:TPU:1, one launch (start us, length us, event | category | flops | bytes accessed | tf_op | source)
XLA Modules:
  0.0 57.3 jit_solution(2394585809679617256)
XLA Ops:
  0.0 53.9 %shard_map.28 = f32[8,256,1024]{2,1,0:T(8,128)S(1)} custom-call(s32[1,4]{1,0:T(1,128)} %flags.1, bf16[1024,256]{1,0:T(8,128)(2,1)} %own.1), custom_call_target="tpu_custom_call" | custom-call | flops 17179869184 | bytes 8388608 | tf_op jit(solution)/shard_map/pallas_call | solution.py:286
  53.9 3.4 %copy.4 = f32[8,256,1024]{2,1,0:T(8,128)} copy(f32[8,256,1024]{2,1,0:T(8,128)S(1)} %shard_map.28) | data formatting | bytes 16777216
